TPU v7x, 32 devices: a whole 2x2x4 slice. The times are simulated.
32 devices in a mesh: groups: 2 (over x), vox: 16 (over z, y, core).
Axes of the slice: x: 2, y: 2, z: 4, core: 2. Of those that a mesh axis runs over, the one named last changes fastest.
Arguments:
- inc_panels: bfloat16 [256, 3, 16384], P(('groups', 'vox')), parts along dimension 0, may hold values from -6 to 6
- contrast: float32 [2, 32768], P(None, ('groups', 'vox')), parts along dimension 1, may hold values from -1.5 to 1.5
- green_table: bfloat16 [27, 2, 192, 192], replicated, may hold values from -0.0625 to 0.0625
- neighbors: int32 [512, 27], P(('groups', 'vox')), parts along dimension 0, may hold values from 0 to 255, as said below
- panel_column: int32 [256], P('groups'), parts along dimension 0, may hold values from 0 to 127, each once
- receiver_voxel: int32 [16384], P(('groups', 'vox')), parts along dimension 0, may hold values from 0 to 16383, as said below
- receiver_owner: int32 [16384], P(('groups', 'vox')), parts along dimension 0, may hold values from 0 to 15, as said below
Outputs:
- applied: bfloat16 [512, 192, 128], P(('groups', 'vox')), parts along dimension 0
- scattered: bfloat16 [32768, 3, 128], P(('groups', 'vox')), parts along dimension 0
There are 2 independent parts, one for each index of `groups`. A program takes and returns all parts, laid end to end along the dimension named above; an argument that names none is the same for every part. Nothing has to cross between parts.
Inputs may be any that keep to these rules, and one draw needn't show every extreme that they name: `neighbors`: blocks lie on a grid whose first dimension counts slabs: blocks s * 16 to s * 16 + 15 form slab s, a layer of 4 x 4 blocks, each taking one cell of the layer (which cell is drawn); entry (b, o) is the block at offset (o // 9 - 1, (o // 3) % 3 - 1, o % 3 - 1) from block b, each coordinate clipped to the grid. `receiver_voxel`: row r names a voxel of device r // 512's own range, from (r // 512) * 1024 up to, not including, (r // 512 + 1) * 1024. `receiver_owner`: the 512 rows of one device name any one owner at most 64 times, and some device names some owner exactly that often; any owner is named by at most 1024 rows in all, and some owner exactly that often.
All inputs are finite; a program needn't handle non-finite values.
Results may differ from a plain program's by a relative error of at most 0.0049.
Values may be sent and summed in bfloat16 or wider, within the bound.
A program may use at most 256 MiB of HBM per device.

v0:
```python
import jax
import jax.numpy as jnp
from jax import lax
from jax.sharding import PartitionSpec as P

BV = 64
HB = 16


def extended_2(array, sides, width):
    for axis, dim in sides:
        count, length = (lax.axis_size(axis), array.shape[dim])
        up = [(i, (i + 1) % count) for i in range(count - 1)]
        down = [(j, i) for i, j in up]
        last = lax.slice_in_dim(array, length - width, length, axis=dim)
        first = lax.slice_in_dim(array, 0, width, axis=dim)
        before = lax.ppermute(last, axis, up)
        after = lax.ppermute(first, axis, down)
        array = jnp.concatenate([before, array, after], axis=dim)
    return array


def arrange_columns(received, panel_column, block_count):
    panel_count = received.shape[0]
    onehot = (panel_column[:, None] == jnp.arange(panel_count, dtype=jnp.int32)[None, :]).astype(
        jnp.bfloat16
    )
    voxel_grid = received.reshape(panel_count, 3, block_count, BV)
    arranged = jnp.einsum("pcbv,pk->bcvk", voxel_grid, onehot, preferred_element_type=jnp.float32)
    return arranged.astype(jnp.bfloat16)


def apply_contrast(fields, contrast):
    block_count = fields.shape[0]
    half_width = fields.shape[3] // 2
    contrast_re = contrast[0].reshape(block_count, 1, BV, 1)
    contrast_im = contrast[1].reshape(block_count, 1, BV, 1)
    real_part = fields[..., :half_width].astype(jnp.float32)
    imag_part = fields[..., half_width:].astype(jnp.float32)
    currents = jnp.concatenate(
        [
            contrast_re * real_part - contrast_im * imag_part,
            contrast_re * imag_part + contrast_im * real_part,
        ],
        axis=3,
    )
    return currents.astype(jnp.bfloat16).reshape(block_count, 3 * BV, 2 * half_width)


def per_device(
    inc_panels, contrast, green_table, neighbors, panel_column, receiver_voxel, receiver_owner
):
    axis_count = lax.axis_size("vox")
    my_index = lax.axis_index("vox")
    vox_dev = contrast.shape[1]
    block_count = vox_dev // BV
    received = lax.all_to_all(inc_panels, "vox", split_axis=2, concat_axis=0, tiled=True)
    fields = arrange_columns(received, panel_column, block_count)
    currents = apply_contrast(fields, contrast)
    extended = extended_2(currents, (("vox", 0),), HB)
    half_width = fields.shape[3] // 2
    width_rows = 3 * BV
    class_count = green_table.shape[0]
    joined_table = green_table.reshape(class_count, 2 * width_rows, width_rows)
    joined_table = joined_table.transpose(1, 0, 2)
    local_index = neighbors - (my_index * block_count - HB)
    gathered = jnp.take(extended, local_index, axis=0)
    total = jnp.einsum("ioj,bojk->bik", joined_table, gathered, preferred_element_type=jnp.float32)
    lower_part = total[:, width_rows:, :]
    green_out = total[:, :width_rows, :] + jnp.concatenate(
        [-lower_part[..., half_width:], lower_part[..., :half_width]], axis=2
    )
    flat_field = fields.reshape(block_count, width_rows, 2 * half_width).astype(jnp.float32)
    applied = (flat_field - green_out).astype(jnp.bfloat16)
    row_count = receiver_voxel.shape[0]
    peak_rows = max(2, (row_count + axis_count - 1) // axis_count)
    send_cap = 2 * peak_rows
    own_cap = 2 * row_count
    local_voxel = receiver_voxel - my_index * vox_dev
    block_of = local_voxel // BV
    within = local_voxel % BV
    row_index = jnp.arange(3, dtype=jnp.int32)[None, :] * BV + within[:, None]
    rows = green_out[block_of[:, None], row_index].astype(jnp.bfloat16)
    owner_ids = jnp.arange(axis_count, dtype=jnp.int32)
    matches = (receiver_owner[:, None] == owner_ids[None, :]).astype(jnp.int32)
    earlier = jnp.cumsum(matches, axis=0) - matches
    send_slot = jnp.sum(earlier * matches, axis=1)
    owner_counts = jnp.sum(matches, axis=0)
    send_buffer = jnp.zeros((axis_count, send_cap, 3, 2 * half_width), jnp.bfloat16)
    send_buffer = send_buffer.at[receiver_owner, send_slot].set(rows)
    tallies = owner_counts.astype(jnp.bfloat16).reshape(axis_count, 1)
    arrived, arrived_counts = (
        lax.all_to_all(send_buffer, "vox", split_axis=0, concat_axis=0, tiled=True),
        lax.all_to_all(tallies, "vox", split_axis=0, concat_axis=0, tiled=True),
    )
    got_counts = arrived_counts.reshape(axis_count).astype(jnp.int32)
    offsets = jnp.cumsum(got_counts) - got_counts
    slot_ids = jnp.arange(send_cap, dtype=jnp.int32)[None, :]
    placement = jnp.where(slot_ids < got_counts[:, None], offsets[:, None] + slot_ids, own_cap)
    scattered = jnp.zeros((own_cap, 3, 2 * half_width), jnp.bfloat16)
    scattered = scattered.at[placement.reshape(-1)].set(
        arrived.reshape(axis_count * send_cap, 3, 2 * half_width), mode="drop"
    )
    return (applied, scattered)


def solution(mesh):
    in_specs = (
        P(("groups", "vox"), None, None),
        P(None, ("groups", "vox")),
        P(),
        P(("groups", "vox"), None),
        P("groups"),
        P(("groups", "vox")),
        P(("groups", "vox")),
    )
    out_specs = (P(("groups", "vox"), None, None), P(("groups", "vox"), None, None))
    return jax.shard_map(
        per_device, mesh=mesh, in_specs=in_specs, out_specs=out_specs, check_vma=False
    )
```

profile of v0, /device:TPU:19, one launch (start us, length us, event | category | flops | bytes accessed | tf_op | source)
XLA Modules:
  0.0 259.7 jit_solution(7196711662594410874)
XLA Ops:
  0.6 17.7 %copy.40 = bf16[8,3,16384]{0,1,2:T(4,128)(2,1)} copy(bf16[8,3,16384]{2,0,1:T(8,128)(2,1)} %param.7) | data formatting | bytes 1572864 | tf_op args[0]
  18.3 19.0 %reshape.283 = bf16[16,2,12288]{2,1,0:T(2,128)(2,1)} reshape(bf16[16384,3,8]{2,1,0:T(4,128)(2,1)} %bitcast.53) | data formatting | bytes 1572864
  37.3 6.5 %all-to-all-start = ((bf16[16,2,12288]{2,1,0:T(2,128)(2,1)}), bf16[16,2,12288]{2,1,0:T(2,128)(2,1)S(1)}, u32[]{:S(2)}, u32[]{:S(2)}) async-start(bf16[16,2,12288]{2,1,0:T(2,128)(2,1)} %reshape.283), calls=%async_computation | async-start | bytes 1572864 | tf_op jit(solution)/shard_map/all_to_all | solution.py:57
  44.0 0.1 reshape.235
  44.2 7.4 %copy.46 = bf16[27,384,192]{1,2,0:T(8,128)(2,1)} copy(bf16[27,384,192]{2,1,0:T(8,128)(2,1)} %bitcast.62) | data formatting | bytes 7962624 | tf_op jit(solution)/shard_map/reshape | solution.py:64
  51.5 1.2 reduce-window.19
  52.7 0.2 slice_reduce_fusion
  52.9 0.2 fusion.19
  53.1 0.7 copy.48
  53.8 9.1 %all-to-all-done = bf16[16,2,12288]{2,1,0:T(2,128)(2,1)S(1)} async-done(((bf16[16,2,12288]{2,1,0:T(2,128)(2,1)}), bf16[16,2,12288]{2,1,0:T(2,128)(2,1)S(1)}, u32[]{:S(2)}, u32[]{:S(2)}) %all-to-all-start) | async-done | bytes 786464 | tf_op jit(solution)/shard_map/all_to_all | solution.py:57
  62.9 5.1 %all-to-all-start.1 = ((bf16[16,1,1]{2,1,0:T(2,128)(2,1)}), bf16[16,1,1]{2,1,0:T(2,128)(2,1)S(1)}, u32[]{:S(2)}, u32[]{:S(2)}) async-start(bf16[16,1,1]{2,1,0:T(2,128)(2,1)} %copy.48), calls=%async_computation.1 | async-start | bytes 16384 | tf_op jit(solution)/shard_map/all_to_all | solution.py:94
  68.0 16.5 %reshape.284 = bf16[16384,3,8]{2,1,0:T(4,128)(2,1)} reshape(bf16[16,2,12288]{2,1,0:T(2,128)(2,1)S(1)} %all-to-all-done) | data formatting | bytes 1572864
  84.6 20.7 %copy.41 = bf16[8,3,16,1024]{3,0,2,1:T(8,128)(2,1)S(1)} copy(bf16[8,3,16,1024]{0,1,3,2:T(4,128)(2,1)} %bitcast.52) | data formatting | bytes 1572864 | tf_op jit(solution)/shard_map/all_to_all | solution.py:57
  105.3 1.0 reshape.225
  106.3 1.1 copy.42
  107.5 0.4 fusion.17
  107.9 0.1 convert_bitcast_fusion
  108.0 0.7 fusion.11
  108.9 1.3 pad_maximum_fusion.1
  110.2 3.3 %collective-permute-start = (bf16[16,192,128]{2,1,0:T(8,128)(2,1)}, bf16[16,192,128]{2,1,0:T(8,128)(2,1)}, u32[]{:S(2)}, u32[]{:S(2)}) collective-permute-start(bf16[16,192,128]{2,1,0:T(8,128)(2,1)} %pad_maximum_fusion.1), channel_id=1, source_target_pairs={{0,1},{1,2},{2,3},{3,4},{4,5},{5,6},{6,7},{7,8},{8,9},{9,10},{10,1... | collective-permute-start | bytes 2359304 | tf_op jit(solution)/shard_map/ppermute | solution.py:17
  113.5 2.1 collective-permute-start.1
  115.6 0.2 fusion.16
  115.8 0.2 reshape.241
  116.1 1.3 copy.43
  117.4 2.8 %copy.47 = f32[16,192,128]{1,2,0:T(8,128)} copy(f32[16,192,128]{2,1,0:T(8,128)} %bitcast.61) | data formatting | bytes 3145728 | tf_op jit(solution)/shard_map/convert_element_type | solution.py:73
  120.3 10.9 %collective-permute-done = bf16[16,192,128]{2,1,0:T(8,128)(2,1)} collective-permute-done((bf16[16,192,128]{2,1,0:T(8,128)(2,1)}, bf16[16,192,128]{2,1,0:T(8,128)(2,1)}, u32[]{:S(2)}, u32[]{:S(2)}) %collective-permute-start) | collective-permute-done | bytes 786464 | tf_op jit(solution)/shard_map/ppermute | solution.py:17
  131.2 1.6 collective-permute-done.1
  132.8 2.2 pad_maximum_fusion
  135.0 15.3 %gather_fusion = bf16[432,192,128]{2,1,0:T(8,128)(2,1)} fusion(bf16[48,192,128]{2,1,0:T(8,128)(2,1)S(1)} %pad_maximum_fusion, s32[1024]{0:T(1024)S(1)} %pad_clamp_fusion), kind=kCustom, calls=%fused_computation | custom fusion | bytes 42469056 | tf_op jit(solution)/shard_map/jit(_take)/gather | solution.py:67
  150.3 21.8 %fusion.5 = f32[16,384,128]{1,2,0:T(8,128)S(1)} fusion(bf16[27,384,192]{1,2,0:T(8,128)(2,1)} %copy.46, bf16[16,27,192,128]{3,2,1,0:T(8,128)(2,1)} %bitcast.55, pred[16,27]{1,0:T(8,128)(4,1)S(1)} %get-tuple-element.16), kind=kOutput, calls=%fused_computation.16 | convolution fusion | flops 8164343808 | bytes 28361136 | tf_op jit(solution)/shard_map/ioj,bojk->bik/dot_general | solution.py:68
  172.1 0.6 slice_negate_fusion
  172.7 1.0 copy-done
  173.7 0.7 subtract_convert_fusion
  174.4 0.6 copy.51
  175.0 8.5 %gather_fusion.1 = bf16[1536,128]{1,0:T(8,128)(2,1)S(1)} fusion(bf16[16,192,128]{2,1,0:T(8,128)(2,1)S(1)} %copy.51, s32[1536]{0:T(1024)S(1)} %reshape.241), kind=kCustom, calls=%fused_computation.1 | custom fusion | bytes 798720 | tf_op jit(solution)/shard_map/gather | solution.py:83
  183.5 0.2 reshape.263
  183.7 0.4 broadcast_in_dim.51
  184.1 19.2 %scatter_fusion = bf16[16,64,3,128]{3,2,1,0:T(4,128)(2,1)S(1)} fusion(bf16[16,64,3,128]{3,2,1,0:T(4,128)(2,1)S(1)} %broadcast_in_dim.51, s32[512]{0:T(512)S(1)} %bitcast.54, bf16[512,3,128]{2,1,0:T(4,128)(2,1)S(1)} %reshape.263), kind=kCustom, calls=%fused_computation.2 | custom fusion | bytes 1183744 | tf_op jit(solution)/shard_map/scatter | solution.py:90
  203.3 1.1 copy.52
  204.4 4.9 %all-to-all-start.2 = ((bf16[16,64,3,128]{3,1,2,0:T(8,128)(2,1)}), bf16[16,64,3,128]{3,1,2,0:T(8,128)(2,1)S(1)}, u32[]{:S(2)}, u32[]{:S(2)}) async-start(bf16[16,64,3,128]{3,1,2,0:T(8,128)(2,1)} %copy.52), calls=%async_computation.2 | async-start | bytes 1572864 | tf_op jit(solution)/shard_map/all_to_all | solution.py:93
  209.4 0.1 reduce.3
  209.5 0.4 convert_reduce_fusion.1
  210.1 1.3 copy.55
  211.3 17.1 %all-to-all-done.2 = bf16[16,64,3,128]{3,1,2,0:T(8,128)(2,1)S(1)} async-done(((bf16[16,64,3,128]{3,1,2,0:T(8,128)(2,1)}), bf16[16,64,3,128]{3,1,2,0:T(8,128)(2,1)S(1)}, u32[]{:S(2)}, u32[]{:S(2)}) %all-to-all-start.2) | async-done | bytes 786464 | tf_op jit(solution)/shard_map/all_to_all | solution.py:93
  228.4 0.7 copy.54
  229.1 0.3 broadcast_in_dim.48
  229.4 29.3 %scatter_fusion.1 = bf16[1024,3,128]{2,1,0:T(4,128)(2,1)S(1)} fusion(bf16[1024,3,128]{2,1,0:T(4,128)(2,1)S(1)} %broadcast_in_dim.48, s32[1024]{0:T(1024)S(1)} %bitcast.68, bf16[1024,3,128]{2,1,0:T(4,128)(2,1)S(1)} %copy.54), kind=kCustom, calls=%fused_computation.3 | custom fusion | bytes 2363392 | tf_op jit(solution)/shard_map/scatter | solution.py:101
  258.7 1.0 copy.56
  (36 shorter events, 0.7 us)
Async XLA Ops:
  18.3 25.5 %copy-start.4 = (f32[2,1024]{1,0:T(2,128)S(1)}, f32[2,1024]{1,0:T(2,128)}, u32[]{:S(2)}) copy-start(f32[2,1024]{1,0:T(2,128)} %param.8) | copy-start | bytes 24580
  18.3 25.7 %copy-start.3 = (s32[16,27]{1,0:T(8,128)S(1)}, s32[16,27]{1,0:T(8,128)}, u32[]{:S(2)}) copy-start(s32[16,27]{1,0:T(8,128)} %param.10) | copy-start | bytes 5188
  37.3 25.6 %all-to-all-start = ((bf16[16,2,12288]{2,1,0:T(2,128)(2,1)}), bf16[16,2,12288]{2,1,0:T(2,128)(2,1)S(1)}, u32[]{:S(2)}, u32[]{:S(2)}) async-start(bf16[16,2,12288]{2,1,0:T(2,128)(2,1)} %reshape.283), calls=%async_computation | async-start | bytes 1572864 | tf_op jit(solution)/shard_map/all_to_all | solution.py:57
  44.1 7.4 %copy-start.2 = (s32[512]{0:T(512)S(1)}, s32[512]{0:T(512)}, u32[]{:S(2)}) copy-start(s32[512]{0:T(512)} %param.13) | copy-start | bytes 6148
  44.1 9.7 %copy-start.5 = (s32[512]{0:T(512)S(1)}, s32[512]{0:T(512)}, u32[]{:S(2)}) copy-start(s32[512]{0:T(512)} %param.12) | copy-start | bytes 6148
  62.9 141.5 %all-to-all-start.1 = ((bf16[16,1,1]{2,1,0:T(2,128)(2,1)}), bf16[16,1,1]{2,1,0:T(2,128)(2,1)S(1)}, u32[]{:S(2)}, u32[]{:S(2)}) async-start(bf16[16,1,1]{2,1,0:T(2,128)(2,1)} %copy.48), calls=%async_computation.1 | async-start | bytes 16384 | tf_op jit(solution)/shard_map/all_to_all | solution.py:94
  105.3 2.2 copy-start.6
  108.8 22.3 %copy-start.1 = (bf16[16,3,64,64]{3,2,1,0:T(8,128)(2,1)}, bf16[16,3,64,64]{3,2,1,0:T(8,128)(2,1)S(1)}, u32[]{:S(2)}) copy-start(bf16[16,3,64,64]{3,2,1,0:T(8,128)(2,1)S(1)} %copy.45) | copy-start | bytes 1179652
  110.2 21.0 %collective-permute-start = (bf16[16,192,128]{2,1,0:T(8,128)(2,1)}, bf16[16,192,128]{2,1,0:T(8,128)(2,1)}, u32[]{:S(2)}, u32[]{:S(2)}) collective-permute-start(bf16[16,192,128]{2,1,0:T(8,128)(2,1)} %pad_maximum_fusion.1), channel_id=1, source_target_pairs={{0,1},{1,2},{2,3},{3,4},{4,5},{5,6},{6,7},{7,8},{8,9},{9,10},{10,1... | collective-permute-start | bytes 2359304 | tf_op jit(solution)/shard_map/ppermute | solution.py:17
  113.5 19.3 %collective-permute-start.1 = (bf16[16,192,128]{2,1,0:T(8,128)(2,1)}, bf16[16,192,128]{2,1,0:T(8,128)(2,1)}, u32[]{:S(2)}, u32[]{:S(2)}) collective-permute-start(bf16[16,192,128]{2,1,0:T(8,128)(2,1)} %pad_maximum_fusion.1), channel_id=1, source_target_pairs={{1,0},{2,1},{3,2},{4,3},{5,4},{6,5},{7,6},{8,7},{9,8},{10,9},{11,1... | collective-permute-start | bytes 2359304 | tf_op jit(solution)/shard_map/ppermute | solution.py:18
  172.1 1.6 copy-start
  204.4 24.0 %all-to-all-start.2 = ((bf16[16,64,3,128]{3,1,2,0:T(8,128)(2,1)}), bf16[16,64,3,128]{3,1,2,0:T(8,128)(2,1)S(1)}, u32[]{:S(2)}, u32[]{:S(2)}) async-start(bf16[16,64,3,128]{3,1,2,0:T(8,128)(2,1)} %copy.52), calls=%async_computation.2 | async-start | bytes 1572864 | tf_op jit(solution)/shard_map/all_to_all | solution.py:93
where the time goes:
time: 263 us; the launch traced here: 260 us
  local copies, waits for them, and re-layouts  168 us (64%)
  waiting for transfers between devices  38.7 us (15%)
  matrix products  22.2 us (8%)
  starting transfers between devices  22 us (8%)
  other arithmetic  7.86 us (3%)
    unnamed x19, local copies, waits for them, and re-layouts  56.5 us
    scatter x1, local copies, waits for them, and re-layouts, per_device(): scattered.at[placement.reshape(-1)]  29.3 us
    dot_general x1, matrix products, per_device(): jnp.einsum('ioj,bojk->bik', joined_table, gathered, preferred_element_typ...  21.8 us
    all_to_all x1, local copies, waits for them, and re-layouts, per_device(): lax.all_to_all(inc_panels, 'vox', split_axis=2, concat_axis=0, tiled=True)  20.7 us
    scatter x2, local copies, waits for them, and re-layouts, per_device(): send_buffer = send_buffer.at[receiver_owner, send_slot].set(rows)  20.3 us
    all_to_all x1, waiting for transfers between devices, per_device(): lax.all_to_all(send_buffer, 'vox', split_axis=0, concat_axis=0, tiled=True)  17.1 us
    gather x1, local copies, waits for them, and re-layouts, per_device(): gathered = jnp.take(extended, local_index, axis=0)  15.3 us
    ppermute x1, waiting for transfers between devices, extended_2(): before = lax.ppermute(last, axis, up)  10.9 us
  transfers between devices with their start and end apart: 5, of which 4 were waited for; matrix products, arithmetic and copies ran while one was open for 50% of the time, Pallas kernels for 0%

commit v1 on v0

v1 whole, which is shorter than its diff:
```python
import functools

import jax
import jax.numpy as jnp
from jax import lax
from jax.experimental import pallas as pl
from jax.experimental.pallas import tpu as pltpu
from jax.sharding import PartitionSpec as P

BV = 64
MESH = pl.DeviceIdType.MESH
F32 = jnp.float32
BF16 = jnp.bfloat16


def dot(a, b, dims=(((1,), (0,)), ((), ()))):
    return lax.dot_general(a, b, dims, preferred_element_type=F32)


def iota(shape, dim):
    return lax.broadcasted_iota(jnp.int32, shape, dim)


def kernel(
    n,
    cap,
    inc_ref,
    table_ref,
    contrast_ref,
    column_ref,
    voxel_ref,
    owner_ref,
    nbr_ref,
    applied_ref,
    scattered_ref,
    recv,
    raw,
    table_own,
    table_far,
    con,
    fields,
    cur,
    lef,
    rig,
    g_own,
    g_far,
    acc,
    green,
    select,
    place,
    send,
    arrived,
    count_out,
    count_in,
    panel_send,
    panel_recv,
    count_send,
    count_recv,
    halo_send,
    halo_recv,
    row_send,
    row_recv,
    local_sem,
):
    me = lax.axis_index("vox")
    panels = recv.shape[0] * recv.shape[2]
    vox = recv.shape[3]
    blocks = vox // BV
    width = fields.shape[2]
    half = width // 2
    rows = fields.shape[1]
    classes = raw.shape[0]
    third = classes // 3
    slots = n * cap
    count = owner_ref.shape[1]
    own_cap = scattered_ref.shape[1]

    def peer(k):
        return lax.rem(me + k, n)

    def remote(src, dst, s, r, device):
        return pltpu.make_async_remote_copy(
            src_ref=src, dst_ref=dst, send_sem=s, recv_sem=r,
            device_id={"vox": device}, device_id_type=MESH,
        )

    def panel_part(d):
        return inc_ref.at[:, :, pl.ds(pl.multiple_of(d * vox, vox), vox)]

    load_table = pltpu.make_async_copy(table_ref, raw, local_sem.at[0])
    load_table.start()
    keep_panels = pltpu.make_async_copy(panel_part(me), recv.at[me], local_sem.at[1])
    keep_panels.start()

    barrier = pltpu.get_barrier_semaphore()

    @pl.loop(1, n)
    def _(k):
        pl.semaphore_signal(barrier, inc=1, device_id={"vox": peer(k)}, device_id_type=MESH)

    pl.semaphore_wait(barrier, n - 1)

    def send_panels(k):
        d = peer(k)
        return remote(panel_part(d), recv.at[me], panel_send.at[d], panel_recv.at[me], d)

    @pl.loop(1, n)
    def _(k):
        send_panels(k).start()

    owner = owner_ref[...]
    matches = (iota((n, count), 0) == owner).astype(F32)
    matches16 = matches.astype(BF16)
    upper = (iota((count, count), 0) < iota((count, count), 1)).astype(F32).astype(BF16)
    earlier = dot(matches16, upper)
    slot = jnp.sum(matches * earlier, axis=0, keepdims=True)
    slot_id = owner * cap + slot.astype(jnp.int32)
    tally = dot(matches16, jnp.ones((count, 128), BF16))
    count_out[...] = jnp.broadcast_to(tally[:, None, :], (n, 8, 128))
    count_in[me] = jnp.zeros((8, 128), F32) + jnp.sum(
        jnp.where(iota((n, 128), 0) == me, tally, 0.0), axis=0, keepdims=True
    )

    def send_count(k):
        d = peer(k)
        return remote(count_out.at[d], count_in.at[me], count_send.at[d], count_recv.at[me], d)

    @pl.loop(1, n)
    def _(k):
        send_count(k).start()

    within = voxel_ref[...] - me * vox
    voxel_hot = (iota((vox, count), 0) == within).astype(F32).astype(BF16)
    step = 256

    for base in range(0, slots, step):
        slot_hot = (iota((step, count), 0) + base == slot_id).astype(F32).astype(BF16)
        select[pl.ds(base, step), :] = dot(slot_hot, voxel_hot, (((1,), (1,)), ((), ()))).astype(BF16)

    for part in range(2):
        line = jnp.broadcast_to(contrast_ref[part : part + 1, :], (128, vox))
        con[part] = line.T

    column = column_ref[...]
    k_index = iota((2 * width, panels), 0)
    plain = k_index == column
    from_im = k_index - width + half == column
    from_re = k_index - width - half == column
    swapped = jnp.where(k_index < width + half, -from_im.astype(F32), from_re.astype(F32))
    order = jnp.where(k_index < width, plain.astype(F32), swapped).T.astype(BF16)

    load_table.wait()

    def join(first, last, target):
        at = 0
        ids = list(range(first, last))
        while ids:
            if len(ids) >= 2:
                a, b = ids[0], ids[1]
                target[:, at : at + 2 * rows] = jnp.concatenate([raw[a], raw[b]], axis=1)
                at += 2 * rows
                ids = ids[2:]
            else:
                pad = target.shape[1] - at - rows
                tail = [raw[ids[0]]]
                if pad:
                    tail.append(jnp.zeros((2 * rows, pad), BF16))
                target[:, at:] = jnp.concatenate(tail, axis=1)
                ids = []

    join(third, 2 * third, table_own)
    far = [o for o in range(classes) if not third <= o < 2 * third]
    for i in range(0, len(far), 2):
        target = 2 * rows * (i // 2)
        table_far[:, target : target + 2 * rows] = jnp.concatenate(
            [raw[far[i]], raw[far[i + 1]]], axis=1
        )
    own_rows = third * rows
    if g_own.shape[0] > own_rows:
        g_own[own_rows:, :] = jnp.zeros((g_own.shape[0] - own_rows, 2 * width), BF16)

    keep_panels.wait()

    @pl.loop(1, n)
    def _(k):
        s = peer(k)
        remote(recv.at[s], recv.at[s], panel_send.at[s], panel_recv.at[s], s).wait_recv()

    for c in range(3):
        got = recv[:, c].astype(F32).reshape(panels, vox).astype(BF16)
        both = dot(got, order, (((0,), (0,)), ((), ())))
        field = both[:, :width]
        current = con[0] * field + con[1] * both[:, width:]
        fields[:, c * BV : (c + 1) * BV, :] = field.reshape(blocks, BV, width).astype(BF16)
        cur[:, c * BV : (c + 1) * BV, :] = current.reshape(blocks, BV, width).astype(BF16)

    def to_right():
        return remote(cur, lef, halo_send.at[0], halo_recv.at[0], me + 1)

    def to_left():
        return remote(cur, rig, halo_send.at[1], halo_recv.at[1], me - 1)

    @pl.when(me < n - 1)
    def _():
        to_right().start()

    @pl.when(me > 0)
    def _():
        to_left().start()

    @pl.when(me == 0)
    def _():
        lef[...] = cur[...]

    @pl.when(me == n - 1)
    def _():
        rig[...] = cur[...]

    def gather(target, at, source, b, o):
        for h in range(2):
            index = lax.rem(nbr_ref[b + h, o], blocks)
            target[at : at + rows, h * width : (h + 1) * width] = source[index]

    @pl.loop(0, blocks // 2)
    def _(pair):
        for i in range(third):
            gather(g_own, i * rows, cur, 2 * pair, third + i)
        acc[pair] = dot(table_own[...], g_own[...])

    @pl.loop(1, n)
    def _(k):
        s = peer(k)
        remote(count_in.at[s], count_in.at[s], count_send.at[s], count_recv.at[s], s).wait_recv()

    free = (cap - count_in[...]).reshape(n * 8, 128).astype(BF16)
    q = iota((n * 8, slots), 0)
    before = jnp.logical_and(
        (q & 7) == 0, (q >> 3) * cap + cap <= iota((n * 8, slots), 1)
    ).astype(F32).astype(BF16)
    skipped = dot(free, before, (((0,), (0,)), ((), ())))[0:1, :].astype(jnp.int32)
    goes_to = iota((1, slots), 1) - skipped
    for base in range(0, own_cap, step):
        place[base : base + step, :] = (
            (iota((step, slots), 0) + base == goes_to).astype(F32).astype(BF16)
        )

    @pl.when(me > 0)
    def _():
        remote(cur, lef, halo_send.at[0], halo_recv.at[0], me - 1).wait_recv()

    @pl.when(me < n - 1)
    def _():
        remote(cur, rig, halo_send.at[1], halo_recv.at[1], me + 1).wait_recv()

    @pl.loop(0, blocks // 2)
    def _(pair):
        for i, o in enumerate(far):
            gather(g_far, i * rows, lef if o < third else rig, 2 * pair, o)
        total = acc[pair] + dot(table_far[...], g_far[...])
        for h in range(2):
            b = 2 * pair + h
            top = total[:rows, h * width : (h + 1) * width]
            low = total[rows:, h * width : (h + 1) * width]
            turned = jnp.concatenate([-low[:, half:], low[:, :half]], axis=1)
            out = top + turned
            applied_ref[b] = (fields[b].astype(F32) - out).astype(BF16)
            for c in range(3):
                green[pl.ds(pl.multiple_of(b * BV, BV), BV), c * width : (c + 1) * width] = out[
                    c * BV : (c + 1) * BV, :
                ].astype(BF16)

    per = step // cap
    for base in range(0, slots, step):
        chosen = dot(select[base : base + step, :], green[...])
        first = base // cap
        for c in range(3):
            send[first : first + per, c] = (
                chosen[:, c * width : (c + 1) * width].reshape(per, cap, width).astype(BF16)
            )

    def send_rows(k):
        d = peer(k)
        return remote(send.at[d], arrived.at[me], row_send.at[d], row_recv.at[me], d)

    keep_rows = pltpu.make_async_copy(send.at[me], arrived.at[me], local_sem.at[2])
    keep_rows.start()

    @pl.loop(1, n)
    def _(k):
        send_rows(k).start()

    keep_rows.wait()

    @pl.loop(1, n)
    def _(k):
        s = peer(k)
        remote(arrived.at[s], arrived.at[s], row_send.at[s], row_recv.at[s], s).wait_recv()

    for c in range(3):
        came = arrived[:, c].reshape(slots, width)
        for base in range(0, own_cap, step):
            scattered_ref[c, base : base + step, :] = dot(
                place[base : base + step, :], came
            ).astype(BF16)

    @pl.loop(1, n)
    def _(k):
        send_panels(k).wait_send()
        send_count(k).wait_send()
        send_rows(k).wait_send()

    @pl.when(me < n - 1)
    def _():
        to_right().wait_send()

    @pl.when(me > 0)
    def _():
        to_left().wait_send()


def per_device(
    n, inc_panels, contrast, green_table, neighbors, panel_column, receiver_voxel, receiver_owner
):
    vox = contrast.shape[1]
    blocks = vox // BV
    per = inc_panels.shape[0]
    width = panel_column.shape[0]
    classes, _, rows, _ = green_table.shape
    count = receiver_voxel.shape[0]
    peak = max(2, (count + n - 1) // n)
    cap = max(16, 2 * peak)
    own_cap = 2 * count
    slots = n * cap
    third = classes // 3

    panels = inc_panels.transpose(1, 0, 2)
    columns = panel_column.reshape(n, per)
    short = -per % 8
    if short:
        panels = jnp.pad(panels, ((0, 0), (0, short), (0, 0)))
        columns = jnp.pad(columns, ((0, 0), (0, short)), constant_values=-4 * width)
    per += short

    own_depth = -(-third * rows // 128) * 128
    far_depth = (classes - third) * rows
    vmem = pl.BlockSpec(memory_space=pltpu.VMEM)
    smem = pl.BlockSpec(memory_space=pltpu.SMEM)
    hbm = pl.BlockSpec(memory_space=pl.ANY)
    dma = pltpu.SemaphoreType.DMA
    block = (blocks, rows, width)
    applied, scattered = pl.pallas_call(
        functools.partial(kernel, n, cap),
        out_shape=(
            jax.ShapeDtypeStruct(block, BF16),
            jax.ShapeDtypeStruct((3, own_cap, width), BF16),
        ),
        in_specs=[hbm, hbm, vmem, vmem, vmem, vmem, smem],
        out_specs=(vmem, vmem),
        scratch_shapes=[
            pltpu.VMEM((n, 3, per, vox), BF16),
            pltpu.VMEM((classes, 2 * rows, rows), BF16),
            pltpu.VMEM((2 * rows, own_depth), BF16),
            pltpu.VMEM((2 * rows, far_depth), BF16),
            pltpu.VMEM((2, vox, width), F32),
            pltpu.VMEM(block, BF16),
            pltpu.VMEM(block, BF16),
            pltpu.VMEM(block, BF16),
            pltpu.VMEM(block, BF16),
            pltpu.VMEM((own_depth, 2 * width), BF16),
            pltpu.VMEM((far_depth, 2 * width), BF16),
            pltpu.VMEM((blocks // 2, 2 * rows, 2 * width), F32),
            pltpu.VMEM((vox, 3 * width), BF16),
            pltpu.VMEM((slots, vox), BF16),
            pltpu.VMEM((own_cap, slots), BF16),
            pltpu.VMEM((n, 3, cap, width), BF16),
            pltpu.VMEM((n, 3, cap, width), BF16),
            pltpu.VMEM((n, 8, 128), F32),
            pltpu.VMEM((n, 8, 128), F32),
            dma((n,)),
            dma((n,)),
            dma((n,)),
            dma((n,)),
            dma((2,)),
            dma((2,)),
            dma((n,)),
            dma((n,)),
            dma((3,)),
        ],
        compiler_params=pltpu.CompilerParams(
            collective_id=0, has_side_effects=True, vmem_limit_bytes=56 * 1024 * 1024
        ),
    )(
        panels,
        green_table.reshape(classes, 2 * rows, rows),
        contrast,
        columns.reshape(1, n * per),
        receiver_voxel.reshape(1, count),
        receiver_owner.reshape(1, count),
        neighbors,
    )
    return applied, scattered.transpose(1, 0, 2)


def solution(mesh):
    both = ("groups", "vox")
    in_specs = (
        P(both, None, None),
        P(None, both),
        P(),
        P(both, None),
        P("groups"),
        P(both),
        P(both),
    )
    out_specs = (P(both, None, None), P(both, None, None))
    return jax.shard_map(
        functools.partial(per_device, mesh.shape["vox"]),
        mesh=mesh, in_specs=in_specs, out_specs=out_specs, check_vma=False,
    )
```

time: 263 us -> 73 us (0.28)
  the two profiles are of different devices: /device:TPU:19 before, /device:TPU:13 now
where the time goes in v1:
time: 73 us; the launch traced here: 72.7 us
  Pallas kernels  67.9 us (93%)
  local copies, waits for them, and re-layouts  4.13 us (6%)
    pallas_call x1, Pallas kernels, per_device(): pl.pallas_call(functools.partial(kernel, n, cap), out_shape=(jax.ShapeDty...  67.9 us
    unnamed x2, local copies, waits for them, and re-layouts  4.13 us

profile of v1, /device:TPU:13, one launch (start us, length us, event | category | flops | bytes accessed | tf_op | source)
XLA Modules:
  0.0 72.7 jit_solution(5460735394336341711)
XLA Ops:
  0.6 67.9 %shard_map.86 = (bf16[16,192,128]{2,1,0:T(8,128)(2,1)}, bf16[3,1024,128]{2,1,0:T(8,128)(2,1)}) custom-call(bf16[3,8,16384]{2,1,0:T(8,128)(2,1)} %bitcast.8, bf16[27,384,192]{2,1,0:T(8,128)(2,1)} %bitcast.6, f32[2,1024]{1,0:T(2,128)} %contrast_ref.1, s32[1,128]{1,0:T(1,128)} %bitcast.11, s32[1,512]{1,0:T(1,128)} %bitcast.9, s32[1,512]{1,0:T(1,128)} %bitcast.10, ...), custom_call_target="tpu_custom_call" | custom-call | tf_op jit(solution)/shard_map/pallas_call | solution.py:351
  68.6 2.1 %copy.11 = bf16[16,192,128]{2,1,0:T(8,128)(2,1)} copy(bf16[16,192,128]{2,1,0:T(8,128)(2,1)} %get-tuple-element.8) | data formatting | bytes 1572864
  70.7 2.1 %copy.12 = bf16[1024,3,128]{2,0,1:T(8,128)(2,1)} copy(bf16[1024,3,128]{2,0,1:T(8,128)(2,1)} %bitcast.7) | data formatting | bytes 1572864

commit v2 on v1

v2 whole, which is shorter than its diff:
```python
import functools

import jax
import jax.numpy as jnp
from jax import lax
from jax.experimental import pallas as pl
from jax.experimental.pallas import tpu as pltpu
from jax.sharding import PartitionSpec as P

BV = 64
CHUNKS = 4
MESH = pl.DeviceIdType.MESH
F32 = jnp.float32
BF16 = jnp.bfloat16


def dot(a, b, dims=(((1,), (0,)), ((), ()))):
    return lax.dot_general(a, b, dims, preferred_element_type=F32)


def iota(shape, dim):
    return lax.broadcasted_iota(jnp.int32, shape, dim)


def kernel(
    n,
    cap,
    inc_ref,
    table_ref,
    contrast_ref,
    column_ref,
    voxel_ref,
    owner_ref,
    nbr_ref,
    applied_out,
    arrived,
    goes_ref,
    recv,
    raw,
    table_own,
    table_far,
    con,
    fields,
    cur,
    lef,
    rig,
    g_even,
    g_odd,
    far_even,
    far_odd,
    acc,
    green,
    select,
    send,
    applied_ref,
    count_out,
    count_in,
    panel_send,
    panel_recv,
    count_send,
    count_recv,
    halo_send,
    halo_recv,
    row_send,
    row_recv,
    local_sem,
):
    me = lax.axis_index("vox")
    panels = n * recv.shape[3]
    chunk = recv.shape[4]
    vox = CHUNKS * chunk
    blocks = vox // BV
    width = fields.shape[2]
    half = width // 2
    rows = fields.shape[1]
    classes = raw.shape[0]
    third = classes // 3
    slots = n * cap
    count = owner_ref.shape[1]

    def peer(k):
        return lax.rem(me + k, n)

    def remote(src, dst, s, r, device):
        return pltpu.make_async_remote_copy(
            src_ref=src, dst_ref=dst, send_sem=s, recv_sem=r,
            device_id={"vox": device}, device_id_type=MESH,
        )

    def panel_part(q, d):
        start = pl.multiple_of(d * vox + q * chunk, chunk)
        return inc_ref.at[:, :, pl.ds(start, chunk)]

    load_table = pltpu.make_async_copy(table_ref, raw, local_sem.at[0])
    load_table.start()

    def keep_panels(q):
        return pltpu.make_async_copy(panel_part(q, me), recv.at[q, me], local_sem.at[2 + q])

    for q in range(CHUNKS):
        keep_panels(q).start()

    owner = owner_ref[...]
    matches = (iota((n, count), 0) == owner).astype(F32)
    matches16 = matches.astype(BF16)
    upper = (iota((count, count), 0) < iota((count, count), 1)).astype(F32).astype(BF16)
    earlier = dot(matches16, upper)
    slot = jnp.sum(matches * earlier, axis=0, keepdims=True)
    slot_id = owner * cap + slot.astype(jnp.int32)
    tally = dot(matches16, jnp.ones((count, 128), BF16))
    count_out[...] = jnp.broadcast_to(tally[:, None, :], (n, 8, 128))
    count_in[me] = jnp.zeros((8, 128), F32) + jnp.sum(
        jnp.where(iota((n, 128), 0) == me, tally, 0.0), axis=0, keepdims=True
    )

    barrier = pltpu.get_barrier_semaphore()

    @pl.loop(1, n)
    def _(k):
        pl.semaphore_signal(barrier, inc=1, device_id={"vox": peer(k)}, device_id_type=MESH)

    pl.semaphore_wait(barrier, n - 1)

    def send_count(k):
        d = peer(k)
        return remote(count_out.at[d], count_in.at[me], count_send.at[d], count_recv.at[me], d)

    @pl.loop(1, n)
    def _(k):
        send_count(k).start()

    def send_panels(q, k):
        d = peer(k)
        return remote(
            panel_part(q, d), recv.at[q, me], panel_send.at[q, d], panel_recv.at[q, me], d
        )

    for q in range(CHUNKS):

        @pl.loop(1, n)
        def _(k):
            send_panels(q, k).start()

    within = voxel_ref[...] - me * vox
    voxel_hot = (iota((vox, count), 0) == within).astype(F32).astype(BF16)
    step = 256

    for base in range(0, slots, step):
        slot_hot = (iota((step, count), 0) + base == slot_id).astype(F32).astype(BF16)
        select[pl.ds(base, step), :] = dot(slot_hot, voxel_hot, (((1,), (1,)), ((), ()))).astype(BF16)

    for part in range(2):
        line = jnp.broadcast_to(contrast_ref[part : part + 1, :], (128, vox))
        con[part] = line.T

    column = column_ref[...]
    k_index = iota((2 * width, panels), 0)
    plain = k_index == column
    from_im = k_index - width + half == column
    from_re = k_index - width - half == column
    swapped = jnp.where(k_index < width + half, -from_im.astype(F32), from_re.astype(F32))
    order = jnp.where(k_index < width, plain.astype(F32), swapped).T.astype(BF16)

    load_table.wait()

    def join(ids, target):
        at = 0
        while ids:
            if len(ids) >= 2:
                a, b = ids[0], ids[1]
                target[:, at : at + 2 * rows] = jnp.concatenate([raw[a], raw[b]], axis=1)
                at += 2 * rows
                ids = ids[2:]
            else:
                pad = target.shape[1] - at - rows
                tail = [raw[ids[0]]]
                if pad:
                    tail.append(jnp.zeros((2 * rows, pad), BF16))
                target[:, at:] = jnp.concatenate(tail, axis=1)
                ids = []

    join(list(range(third, 2 * third)), table_own)
    join(list(range(third)) + list(range(2 * third, classes)), table_far)
    depth = third * rows
    for target in (g_even, g_odd):
        if target.shape[0] > depth:
            target[depth:, :] = jnp.zeros((target.shape[0] - depth, 2 * width), BF16)

    part_blocks = blocks // CHUNKS

    def of_part(ref, q):
        return ref.at[pl.ds(q * part_blocks, part_blocks)]

    def to_right(q):
        return remote(
            of_part(cur, q), of_part(lef, q), halo_send.at[0, q], halo_recv.at[0, q], me + 1
        )

    def to_left(q):
        return remote(
            of_part(cur, q), of_part(rig, q), halo_send.at[1, q], halo_recv.at[1, q], me - 1
        )

    for q in range(CHUNKS):
        keep_panels(q).wait()

        @pl.loop(1, n)
        def _(k):
            p = peer(k)
            remote(
                recv.at[q, p], recv.at[q, p], panel_send.at[q, p], panel_recv.at[q, p], p
            ).wait_recv()

        v = slice(q * chunk, (q + 1) * chunk)
        z = slice(q * part_blocks, (q + 1) * part_blocks)
        for c in range(3):
            got = recv[q, :, c].astype(F32).reshape(panels, chunk).astype(BF16)
            both = dot(got, order, (((0,), (0,)), ((), ())))
            field = both[:, :width]
            current = con[0, v, :] * field + con[1, v, :] * both[:, width:]
            shape = (part_blocks, BV, width)
            fields[z, c * BV : (c + 1) * BV, :] = field.reshape(shape).astype(BF16)
            cur[z, c * BV : (c + 1) * BV, :] = current.reshape(shape).astype(BF16)

        @pl.when(me < n - 1)
        def _():
            to_right(q).start()

        @pl.when(me > 0)
        def _():
            to_left(q).start()

    @pl.when(me == 0)
    def _():
        lef[...] = cur[...]

    @pl.when(me == n - 1)
    def _():
        rig[...] = cur[...]

    pairs = blocks // 2

    pairs = blocks // 2

    def gather(target, sources, pair):
        at = 0
        for source, first in sources:
            for i in range(third):
                for h in range(2):
                    index = lax.rem(nbr_ref[2 * pair + h, first + i], blocks)
                    target[at : at + rows, h * width : (h + 1) * width] = source[index]
                at += rows

    def multiply(table, even, odd, sources, use):
        gather(even, sources, 0)

        @pl.loop(0, pairs // 2)
        def _(t):
            gather(odd, sources, 2 * t + 1)
            use(2 * t, dot(table[...], even[...]))
            gather(even, sources, jnp.minimum(2 * t + 2, pairs - 1))
            use(2 * t + 1, dot(table[...], odd[...]))

    def keep(pair, product):
        acc[pair] = product

    multiply(table_own, g_even, g_odd, [(cur, third)], keep)

    @pl.loop(1, n)
    def _(k):
        s = peer(k)
        remote(count_in.at[s], count_in.at[s], count_send.at[s], count_recv.at[s], s).wait_recv()

    free = (cap - count_in[...]).reshape(n * 8, 128).astype(BF16)
    q = iota((n * 8, slots), 0)
    before = jnp.logical_and(
        (q & 7) == 0, (q >> 3) * cap + cap <= iota((n * 8, slots), 1)
    ).astype(F32).astype(BF16)
    skipped = dot(free, before, (((0,), (0,)), ((), ())))[0:1, :].astype(jnp.int32)
    goes_ref[...] = jnp.broadcast_to(iota((1, slots), 1) - skipped, goes_ref.shape)

    @pl.when(me > 0)
    def _():
        for q in range(CHUNKS):
            remote(
                of_part(cur, q), of_part(lef, q), halo_send.at[0, q], halo_recv.at[0, q], me - 1
            ).wait_recv()

    @pl.when(me < n - 1)
    def _():
        for q in range(CHUNKS):
            remote(
                of_part(cur, q), of_part(rig, q), halo_send.at[1, q], halo_recv.at[1, q], me + 1
            ).wait_recv()

    def finish(pair, product):
        total = acc[pair] + product
        for h in range(2):
            b = 2 * pair + h
            top = total[:rows, h * width : (h + 1) * width]
            low = total[rows:, h * width : (h + 1) * width]
            turned = jnp.concatenate([-low[:, half:], low[:, :half]], axis=1)
            out = top + turned
            applied_ref[b] = (fields[b].astype(F32) - out).astype(BF16)
            for c in range(3):
                green[pl.ds(pl.multiple_of(b * BV, BV), BV), c * width : (c + 1) * width] = out[
                    c * BV : (c + 1) * BV, :
                ].astype(BF16)

    multiply(table_far, far_even, far_odd, [(lef, 0), (rig, 2 * third)], finish)

    give_applied = pltpu.make_async_copy(applied_ref, applied_out, local_sem.at[2 + CHUNKS])
    give_applied.start()

    def send_rows(d):
        return remote(send.at[d], arrived.at[me], row_send.at[d], row_recv.at[me], d)

    per = step // cap
    for base in range(0, slots, step):
        chosen = dot(select[base : base + step, :], green[...])
        first = base // cap
        for c in range(3):
            send[first : first + per, c] = (
                chosen[:, c * width : (c + 1) * width].reshape(per, cap, width).astype(BF16)
            )

        @pl.loop(first, first + per)
        def _(d):
            @pl.when(d != me)
            def _():
                send_rows(d).start()

    keep_rows = pltpu.make_async_copy(send.at[me], arrived.at[me], local_sem.at[1])
    keep_rows.start()
    keep_rows.wait()

    @pl.loop(1, n)
    def _(k):
        s = peer(k)
        remote(arrived.at[s], arrived.at[s], row_send.at[s], row_recv.at[s], s).wait_recv()

    give_applied.wait()

    @pl.loop(1, n)
    def _(k):
        for q in range(CHUNKS):
            send_panels(q, k).wait_send()
        send_count(k).wait_send()
        send_rows(peer(k)).wait_send()

    @pl.when(me < n - 1)
    def _():
        for q in range(CHUNKS):
            to_right(q).wait_send()

    @pl.when(me > 0)
    def _():
        for q in range(CHUNKS):
            to_left(q).wait_send()


def place_rows(
    arrived_in, applied_in, goes_ref, applied_out, scattered_out, arrived, applied, scattered, sem
):
    n, _, cap, width = arrived.shape
    own_cap = scattered.shape[1]
    step = 256
    load = pltpu.make_async_copy(arrived_in, arrived, sem.at[0])
    load.start()
    load_applied = pltpu.make_async_copy(applied_in, applied, sem.at[1])
    load_applied.start()
    give_applied = pltpu.make_async_copy(applied, applied_out, sem.at[2])
    goes_to = goes_ref[0:1, :]
    load.wait()
    came = [arrived[:, c].reshape(n * cap, width) for c in range(3)]
    given = []
    for i, base in enumerate(range(0, own_cap, step)):
        hot = (iota((step, n * cap), 0) + base == goes_to).astype(F32).astype(BF16)
        for c in range(3):
            scattered[c, base : base + step, :] = dot(hot, came[c]).astype(BF16)
        part = pl.ds(base, step)
        given.append(
            pltpu.make_async_copy(
                scattered.at[:, part, :], scattered_out.at[:, part, :], sem.at[3 + i]
            )
        )
        given[-1].start()
        if i == 0:
            load_applied.wait()
            give_applied.start()
    give_applied.wait()
    for copy in given:
        copy.wait()


def per_device(
    n, inc_panels, contrast, green_table, neighbors, panel_column, receiver_voxel, receiver_owner
):
    vox = contrast.shape[1]
    blocks = vox // BV
    per = inc_panels.shape[0]
    width = panel_column.shape[0]
    classes, _, rows, _ = green_table.shape
    count = receiver_voxel.shape[0]
    peak = max(2, (count + n - 1) // n)
    cap = max(16, 2 * peak)
    own_cap = 2 * count
    slots = n * cap
    third = classes // 3

    panels = inc_panels.transpose(1, 0, 2)
    columns = panel_column.reshape(n, per)
    short = -per % 8
    if short:
        panels = jnp.pad(panels, ((0, 0), (0, short), (0, 0)))
        columns = jnp.pad(columns, ((0, 0), (0, short)), constant_values=-4 * width)
    per += short

    depth = -(-third * rows // 128) * 128
    far_depth = (classes - third) * rows
    vmem = pl.BlockSpec(memory_space=pltpu.VMEM)
    smem = pl.BlockSpec(memory_space=pltpu.SMEM)
    hbm = pl.BlockSpec(memory_space=pl.ANY)
    dma = pltpu.SemaphoreType.DMA
    block = (blocks, rows, width)
    applied, arrived, goes_to = pl.pallas_call(
        functools.partial(kernel, n, cap),
        out_shape=(
            jax.ShapeDtypeStruct(block, BF16),
            jax.ShapeDtypeStruct((n, 3, cap, width), BF16),
            jax.ShapeDtypeStruct((8, slots), jnp.int32),
        ),
        in_specs=[hbm, hbm, vmem, vmem, vmem, vmem, smem],
        out_specs=(hbm, hbm, vmem),
        scratch_shapes=[
            pltpu.VMEM((CHUNKS, n, 3, per, vox // CHUNKS), BF16),
            pltpu.VMEM((classes, 2 * rows, rows), BF16),
            pltpu.VMEM((2 * rows, depth), BF16),
            pltpu.VMEM((2 * rows, far_depth), BF16),
            pltpu.VMEM((2, vox, width), F32),
            pltpu.VMEM(block, BF16),
            pltpu.VMEM(block, BF16),
            pltpu.VMEM(block, BF16),
            pltpu.VMEM(block, BF16),
            pltpu.VMEM((depth, 2 * width), BF16),
            pltpu.VMEM((depth, 2 * width), BF16),
            pltpu.VMEM((far_depth, 2 * width), BF16),
            pltpu.VMEM((far_depth, 2 * width), BF16),
            pltpu.VMEM((blocks // 2, 2 * rows, 2 * width), F32),
            pltpu.VMEM((vox, 3 * width), BF16),
            pltpu.VMEM((slots, vox), BF16),
            pltpu.VMEM((n, 3, cap, width), BF16),
            pltpu.VMEM(block, BF16),
            pltpu.VMEM((n, 8, 128), F32),
            pltpu.VMEM((n, 8, 128), F32),
            dma((CHUNKS, n)),
            dma((CHUNKS, n)),
            dma((n,)),
            dma((n,)),
            dma((2, CHUNKS)),
            dma((2, CHUNKS)),
            dma((n,)),
            dma((n,)),
            dma((3 + CHUNKS,)),
        ],
        compiler_params=pltpu.CompilerParams(
            collective_id=0, has_side_effects=True, vmem_limit_bytes=56 * 1024 * 1024
        ),
    )(
        panels,
        green_table.reshape(classes, 2 * rows, rows),
        contrast,
        columns.reshape(1, n * per),
        receiver_voxel.reshape(1, count),
        receiver_owner.reshape(1, count),
        neighbors,
    )
    applied, scattered = pl.pallas_call(
        place_rows,
        out_shape=(
            jax.ShapeDtypeStruct(block, BF16),
            jax.ShapeDtypeStruct((3, own_cap, width), BF16),
        ),
        in_specs=[hbm, hbm, vmem],
        out_specs=(hbm, hbm),
        scratch_shapes=[
            pltpu.VMEM((n, 3, cap, width), BF16),
            pltpu.VMEM(block, BF16),
            pltpu.VMEM((3, own_cap, width), BF16),
            dma((3 + own_cap // 256,)),
        ],
        compiler_params=pltpu.CompilerParams(vmem_limit_bytes=56 * 1024 * 1024),
    )(arrived, applied, goes_to)
    return applied, scattered.transpose(1, 0, 2)


def solution(mesh):
    both = ("groups", "vox")
    in_specs = (
        P(both, None, None),
        P(None, both),
        P(),
        P(both, None),
        P("groups"),
        P(both),
        P(both),
    )
    out_specs = (P(both, None, None), P(both, None, None))
    return jax.shard_map(
        functools.partial(per_device, mesh.shape["vox"]),
        mesh=mesh, in_specs=in_specs, out_specs=out_specs, check_vma=False,
    )
```

time: 73 us -> 68.1 us (0.933); the launches traced: 72.7 us -> 66.7 us
  local copies, waits for them, and re-layouts: 4.13 us -> 0 us
  Pallas kernels: 67.9 us -> 66.1 us
    pallas_call x1, Pallas kernels: 67.9 us -> 61.5 us  [per_device(): pl.pallas_call(functools.partial(kernel, n, cap), out_shape=(jax.ShapeDty...]
    pallas_call x0 -> x1, Pallas kernels: none -> 4.61 us  [per_device(): pl.pallas_call(place_rows, out_shape=(jax.ShapeDtypeStruct(block, BF16),...]
    unnamed x2 -> x0, local copies, waits for them, and re-layouts: 4.13 us -> none
where the time goes in v2:
time: 68.1 us; the launch traced here: 66.7 us
  Pallas kernels  66.1 us (97%)
    pallas_call x1, Pallas kernels, per_device(): pl.pallas_call(functools.partial(kernel, n, cap), out_shape=(jax.ShapeDty...  61.5 us
    pallas_call x1, Pallas kernels, per_device(): pl.pallas_call(place_rows, out_shape=(jax.ShapeDtypeStruct(block, BF16),...  4.61 us

profile of v2, /device:TPU:13, one launch (start us, length us, event | category | flops | bytes accessed | tf_op | source)
XLA Modules:
  0.0 66.7 jit_solution(3979898500758168030)
XLA Ops:
  0.6 61.5 %shard_map.86 = (bf16[16,192,128]{2,1,0:T(8,128)(2,1)}, bf16[16,3,64,128]{3,2,1,0:T(8,128)(2,1)}, s32[8,1024]{1,0:T(8,128)}) custom-call(bf16[3,8,16384]{2,1,0:T(8,128)(2,1)} %bitcast.7, bf16[27,384,192]{2,1,0:T(8,128)(2,1)} %bitcast.6, f32[2,1024]{1,0:T(2,128)} %contrast_ref.1, s32[1,128]{1,0:T(1,128)} %bitcast.10, s32[1,512]{1,0:T(1,128)} %bitcast.8, ...), custom_call_target="tpu_custom_call" | custom-call | tf_op jit(solution)/shard_map/pallas_call | solution.py:426
  62.1 4.6 %shard_map.87 = (bf16[16,192,128]{2,1,0:T(8,128)(2,1)}, bf16[3,1024,128]{2,1,0:T(8,128)(2,1)}) custom-call(bf16[16,3,64,128]{3,2,1,0:T(8,128)(2,1)} %get-tuple-element.7.arrived_in, bf16[16,192,128]{2,1,0:T(8,128)(2,1)} %get-tuple-element.8.applied_in, s32[8,1024]{1,0:T(8,128)} %get-tuple-element.9.goes_ref), custom_call_target="tpu_custom_call" | custom-call | tf_op jit(solution)/shard_map/pallas_call | solution.py:478

commit v3 on v2

--- a/solution.py
+++ b/solution.py
@@ -316,11 +316,13 @@
         return remote(send.at[d], arrived.at[me], row_send.at[d], row_recv.at[me], d)
 
     per = step // cap
-    for base in range(0, slots, step):
-        chosen = dot(select[base : base + step, :], green[...])
-        first = base // cap
+    turns = slots // step
+    for turn in range(turns):
+        first = lax.rem(me // per + turn + 1, turns) * per
+        base = pl.multiple_of(first * cap, step)
+        chosen = dot(select[pl.ds(base, step), :], green[...])
         for c in range(3):
-            send[first : first + per, c] = (
+            send[pl.ds(first, per), c] = (
                 chosen[:, c * width : (c + 1) * width].reshape(per, cap, width).astype(BF16)
             )
 

time: 68.1 us -> 67.5 us (level)
  no operation moved by 1% of the time
where the time goes in v3:
time: 67.5 us; the launch traced here: 66.7 us
  Pallas kernels  66 us (98%)
    pallas_call x1, Pallas kernels, per_device(): pl.pallas_call(functools.partial(kernel, n, cap), out_shape=(jax.ShapeDty...  61.4 us
    pallas_call x1, Pallas kernels, per_device(): pl.pallas_call(place_rows, out_shape=(jax.ShapeDtypeStruct(block, BF16),...  4.61 us

profile of v3, /device:TPU:13, one launch (start us, length us, event | category | flops | bytes accessed | tf_op | source)
XLA Modules:
  0.0 66.7 jit_solution(678091017777054230)
XLA Ops:
  0.6 61.4 %shard_map.86 = (bf16[16,192,128]{2,1,0:T(8,128)(2,1)}, bf16[16,3,64,128]{3,2,1,0:T(8,128)(2,1)}, s32[8,1024]{1,0:T(8,128)}) custom-call(bf16[3,8,16384]{2,1,0:T(8,128)(2,1)} %bitcast.7, bf16[27,384,192]{2,1,0:T(8,128)(2,1)} %bitcast.6, f32[2,1024]{1,0:T(2,128)} %contrast_ref.1, s32[1,128]{1,0:T(1,128)} %bitcast.10, s32[1,512]{1,0:T(1,128)} %bitcast.8, ...), custom_call_target="tpu_custom_call" | custom-call | tf_op jit(solution)/shard_map/pallas_call | solution.py:428
  62.1 4.6 %shard_map.87 = (bf16[16,192,128]{2,1,0:T(8,128)(2,1)}, bf16[3,1024,128]{2,1,0:T(8,128)(2,1)}) custom-call(bf16[16,3,64,128]{3,2,1,0:T(8,128)(2,1)} %get-tuple-element.7.arrived_in, bf16[16,192,128]{2,1,0:T(8,128)(2,1)} %get-tuple-element.8.applied_in, s32[8,1024]{1,0:T(8,128)} %get-tuple-element.9.goes_ref), custom_call_target="tpu_custom_call" | custom-call | tf_op jit(solution)/shard_map/pallas_call | solution.py:480
